TPU v7x, 128 devices: a whole 4x4x4 slice. The times are simulated.
128 devices in a mesh: seq: 32 (over z_lo, y, x), head: 4 (over z_hi, core).
Axes of the slice: x: 4, y: 4, z: 4 (z_hi: 2, z_lo: 2; z = z_hi * 2 + z_lo), core: 2. Of those that a mesh axis runs over, the one named last changes fastest.
Arguments:
- row_queries: bfloat16 [32768, 2048], P('seq', 'head'), may hold values from -200 to 200
- row_keys: bfloat16 [32768, 2048], P('seq', 'head'), may hold values from -6 to 6
- row_values: bfloat16 [32768, 2048], P('seq', 'head'), may hold values from -6 to 6
- residual_in: bfloat16 [32768, 4096], P(('seq', 'head')), may hold values from -6 to 6
- out_weight: bfloat16 [2048, 4096], P('head', 'seq'), may hold values from -0.25 to 0.25
- norm_gain: float32 [4096], replicated, may hold values from 0.1 to 1.9
- qkv_weight: bfloat16 [4096, 16, 3, 128], P('seq', 'head'), may hold values from -4 to 4
Outputs:
- residual_out: bfloat16 [32768, 4096], P(('seq', 'head'))
- column_out: bfloat16 [32768, 2048], P('seq', 'head')
All inputs are finite; a program needn't handle non-finite values.
Results may differ from a plain program's by a relative error of at most 0.0091.
Values may be sent and summed in bfloat16 or wider, within the bound.
A program may use at most 128 MiB of HBM per device.

v0:
```python
import jax
import jax.numpy as jnp
from jax import lax
from jax.sharding import PartitionSpec as P

HD = 128
COLS = 512


epsilon = 1e-05


def passed_along(array, axis, by):
    size = lax.axis_size(axis)
    pairs = [(i, i + by) for i in range(size) if 0 <= i + by < size]
    return lax.ppermute(array, axis, pairs)


def band_block(queries, keys, values, has_prev):
    width = queries.shape[0]
    scores = jnp.einsum("qhd,khd->hqk", queries, keys, preferred_element_type=jnp.float32) * HD ** (
        -0.5
    )
    query_col = jnp.arange(width, dtype=jnp.int32)[:, None]
    key_col = jnp.arange(2 * width, dtype=jnp.int32)[None, :]
    allowed = jnp.where(
        key_col < width, (key_col > query_col) & has_prev, key_col - width <= query_col
    )
    scores = jnp.where(allowed[None], scores, -jnp.inf)
    shifted = jnp.exp(scores - jnp.max(scores, -1, keepdims=True))
    weights = (shifted / jnp.sum(shifted, -1, keepdims=True)).astype(jnp.bfloat16)
    return jnp.einsum("hqk,khd->qhd", weights, values, preferred_element_type=jnp.float32).astype(
        jnp.bfloat16
    )


def normalize(stream_bf, norm_gain):
    stream = stream_bf.astype(jnp.float32)
    center = stream - jnp.mean(stream, -1, keepdims=True)
    variance = jnp.mean(center * center, -1, keepdims=True)
    return (center * lax.rsqrt(variance + epsilon) * norm_gain).astype(jnp.bfloat16)


def column_block(block):
    queries = block[..., :HD]
    keys = block[..., HD : 2 * HD]
    values = block[..., 2 * HD :]
    scores = jnp.einsum(
        "rchd,schd->chrs", queries, keys, preferred_element_type=jnp.float32
    ) * HD ** (-0.5)
    height = block.shape[0]
    allowed = (
        jnp.arange(height, dtype=jnp.int32)[None, :] <= jnp.arange(height, dtype=jnp.int32)[:, None]
    )
    scores = jnp.where(allowed[None, None], scores, -jnp.inf)
    shifted = jnp.exp(scores - jnp.max(scores, -1, keepdims=True))
    weights = (shifted / jnp.sum(shifted, -1, keepdims=True)).astype(jnp.bfloat16)
    return jnp.einsum(
        "chrs,schd->rchd", weights, values, preferred_element_type=jnp.float32
    ).astype(jnp.bfloat16)


def per_device(row_queries, row_keys, row_values, residual_in, out_weight, norm_gain, qkv_weight):
    positions = row_queries.shape[0]
    features = row_queries.shape[1]
    groups = features // HD
    slab_rows = positions // COLS
    key_back, value_back = passed_along((row_keys[-COLS:], row_values[-COLS:]), "seq", 1)
    all_keys = jnp.concatenate([key_back, row_keys], 0).reshape(-1, groups, HD)
    all_values = jnp.concatenate([value_back, row_values], 0).reshape(-1, groups, HD)
    first_row = lax.axis_index("seq") * slab_rows
    pieces = []
    for line in range(slab_rows):
        query_row = row_queries[line * COLS : (line + 1) * COLS].reshape(COLS, groups, HD)
        key_rows = all_keys[line * COLS : (line + 2) * COLS]
        value_rows = all_values[line * COLS : (line + 2) * COLS]
        pieces.append(
            band_block(query_row, key_rows, value_rows, first_row + line > 0).reshape(
                COLS, features
            )
        )
    row_out = jnp.concatenate(pieces, 0)
    full_out = lax.all_gather(out_weight, "seq", axis=1, tiled=True)
    share = residual_in.shape[0]
    offset = lax.axis_index("head") * share
    terms = jnp.dot(row_out, full_out, preferred_element_type=jnp.float32)
    own_terms = lax.dynamic_slice_in_dim(terms, offset, share, 0) + residual_in.astype(jnp.float32)
    terms = lax.dynamic_update_slice_in_dim(terms, own_terms, offset, 0)
    stream_all = lax.psum(terms, "head").astype(jnp.bfloat16)
    normed_all = normalize(stream_all, norm_gain)
    residual_out = lax.dynamic_slice_in_dim(stream_all, offset, share, 0)
    piece = lax.all_gather(qkv_weight, "seq", axis=0, tiled=True)
    flat = piece.reshape(piece.shape[0], -1)
    projected = jnp.dot(normed_all, flat, preferred_element_type=jnp.float32)
    column_qkv = projected.astype(jnp.bfloat16).reshape(slab_rows, COLS, groups, 3 * HD)
    attended = column_block(
        lax.all_to_all(column_qkv, "seq", split_axis=1, concat_axis=0, tiled=True)
    )
    restored = lax.all_to_all(attended, "seq", split_axis=0, concat_axis=1, tiled=True)
    return (residual_out, restored.reshape(positions, features))


def solution(mesh):
    placed = (
        P("seq", "head"),
        P("seq", "head"),
        P("seq", "head"),
        P(("seq", "head"), None),
        P("head", "seq"),
        P(),
        P("seq", "head", None, None),
    )
    return jax.shard_map(
        per_device,
        mesh=mesh,
        in_specs=placed,
        out_specs=(P(("seq", "head"), None), P("seq", "head")),
        check_vma=False,
    )
```

profile of v0, /device:TPU:1, one launch (start us, length us, event | category | flops | bytes accessed | tf_op | source)
XLA Modules:
  0.0 712.7 jit_solution(7089954354162998214)
XLA Ops:
  7.2 0.0 copy-start.1
  7.2 0.0 all-gather.3.cloned.1.call-start
  7.2 0.7 all-gather.3.cloned.1.call-update
  7.9 0.0 all-gather.5.cloned.1.call-start
  8.0 1.5 copy.36
  9.5 0.0 copy-start.2
  9.5 0.9 slice.54
  10.4 4.8 collective-permute-start.1
  15.2 1.9 slice.41
  17.0 3.0 collective-permute-start
  20.1 1.0 copy.48
  21.1 0.0 all-gather.5.cloned.1.call-update
  21.1 1.3 copy.61
  22.5 2.3 fusion.80
  24.7 2.1 copy.63
  26.8 2.3 fusion.34
  29.1 2.0 fusion.27
  31.1 6.2 fusion.81
  37.3 5.1 fusion.32
  42.4 1.0 copy.62
  43.4 1.1 pad_maximum_fusion.1
  44.5 0.5 copy.35
  45.1 1.1 pad_maximum_fusion
  46.2 7.6 %fusion.82 = (f32[4,512]{1,0:T(4,128)S(1)}, f32[4,512,1024]{1,2,0:T(8,128)}) fusion(pred[512,1024]{0,1:T(8,128)(4,1)} %get-tuple-element.4, bf16[1024,4,128]{0,2,1:T(8,128)(2,1)S(1)} %bitcast.63, bf16[512,4,128]{0,2,1:T(8,128)(2,1)} %bitcast.64), kind=kOutput, calls=%fused_computation.82 | convolution fusion | flops 545260544 | bytes 10493952 | tf_op jit(solution)/shard_map/sub | solution.py:30
  53.8 4.2 fusion.33
  58.0 82.5 %all-gather.3.cloned.1.call-done = bf16[512,4096]{1,0:T(8,128)(2,1)} async-done(((bf16[512,128]{1,0:T(8,128)(2,1)}), bf16[512,4096]{1,0:T(8,128)(2,1)}) %all-gather.3.cloned.1.call-update) | async-done | bytes 4194320 | tf_op jit(solution)/shard_map/all_gather | solution.py:83
  140.6 10.5 %fusion.41 = f32[1024,4096]{1,0:T(8,128)} fusion(bf16[512,4096]{1,0:T(8,128)(2,1)} %all-gather.3.cloned.1.call-done, bf16[512,512]{0,1:T(8,128)(2,1)S(1)} %bitcast.66, bf16[512,512]{0,1:T(8,128)(2,1)S(1)} %bitcast.67), kind=kOutput, calls=%fused_computation.57 | convolution fusion | flops 4297064448 | bytes 22020096 | tf_op jit(solution)/shard_map/dot_general | solution.py:86
  151.1 4.9 add_dynamic-update-slice_fusion
  156.0 430.2 %all-reduce.1 = bf16[1024,4096]{1,0:T(8,128)(2,1)} all-reduce(f32[1024,4096]{1,0:T(8,128)} %add_dynamic-update-slice_fusion), channel_id=1, replica_groups=mesh['seq'=32,'head'=4] {'head'}, use_global_device_ids=true, to_apply=%region_4.5 | all-reduce | flops 4194304 | bytes 25165824 | tf_op jit(solution)/shard_map/psum | solution.py:89
  586.1 4.7 convert_reduce_fusion
  590.8 1.1 copy-done
  591.9 2.3 fusion.5
  594.2 0.0 all-gather.5.cloned.1.call-done
  594.2 19.4 %fusion.23 = bf16[1024,1536]{1,0:T(8,128)(2,1)} fusion(bf16[4096,1536]{0,1:T(8,128)(2,1)} %bitcast.65, bf16[1024,4096]{1,0:T(8,128)(2,1)} %all-reduce.1, f32[4096]{0:T(1024)S(1)} %copy-done.7, f32[1024]{0:T(1024)S(1)} %add_rsqrt_fusion, f32[1024]{0:T(1024)S(1)} %broadcast_multiply_fusion), kind=kOutput, calls=%fused_computation.31 | convolution fusion | flops 12907446272 | bytes 24141824 | tf_op jit(solution)/shard_map/dot_general | solution.py:94
  613.6 5.0 reshape.169
  618.6 2.7 copy.49
  621.4 6.3 all-to-all-start
  627.7 38.8 %all-to-all-done = bf16[2,512,4,384]{3,2,0,1:T(4,128)(2,1)S(1)} async-done(((bf16[2,512,4,384]{3,2,0,1:T(4,128)(2,1)}), bf16[2,512,4,384]{3,2,0,1:T(4,128)(2,1)S(1)}, u32[]{:S(2)}, u32[]{:S(2)}) %all-to-all-start) | async-done | bytes 3145760 | tf_op jit(solution)/shard_map/all_to_all | solution.py:97
  666.5 5.0 copy.72
  671.5 6.4 all_to_all.27
  677.9 0.9 fusion.83
  678.7 2.0 fusion.31
  680.8 3.0 copy.52
  683.8 5.7 all-to-all-start.1
  689.5 3.1 constant_dynamic-slice_fusion
  692.7 11.6 %all-to-all-done.1 = bf16[64,16,4,128]{3,2,1,0:T(4,128)(2,1)S(1)} async-done(((bf16[64,16,4,128]{3,2,1,0:T(4,128)(2,1)}), bf16[64,16,4,128]{3,2,1,0:T(4,128)(2,1)S(1)}, u32[]{:S(2)}, u32[]{:S(2)}) %all-to-all-start.1) | async-done | bytes 1048608 | tf_op jit(solution)/shard_map/all_to_all | solution.py:99
  704.3 0.5 copy.53
  704.7 1.2 copy.73
  (22 shorter events, 0.1 us)
Async XLA Ops:
  7.2 14.0 %copy-start.1 = (bf16[1024,512]{1,0:T(8,128)(2,1)S(1)}, bf16[1024,512]{1,0:T(8,128)(2,1)}, u32[]{:S(2)}) copy-start(bf16[1024,512]{1,0:T(8,128)(2,1)} %param.9) | copy-start | bytes 3145732
  7.2 12.9 %copy-start.6 = (bf16[128,4,3,128]{3,1,2,0:T(4,128)(2,1)S(1)}, bf16[128,4,3,128]{3,1,2,0:T(4,128)(2,1)}, u32[]{:S(2)}) copy-start(bf16[128,4,3,128]{3,1,2,0:T(4,128)(2,1)} %param.13) | copy-start | bytes 1179652
  7.2 133.4 %all-gather.3.cloned.1.call-start = ((), (), s32[]{:S(2)}) async-start(), calls=%async_computation.2 | async-start | bytes 4325376 | tf_op jit(solution)/shard_map/all_gather | solution.py:83
  7.9 586.3 %all-gather.5.cloned.1.call-start = ((), (), s32[]{:S(2)}) async-start(), calls=%async_computation.3 | async-start | bytes 12976128 | tf_op jit(solution)/shard_map/all_gather | solution.py:92
  9.5 17.3 %copy-start.2 = (bf16[1024,512]{1,0:T(8,128)(2,1)S(1)}, bf16[1024,512]{1,0:T(8,128)(2,1)}, u32[]{:S(2)}) copy-start(bf16[1024,512]{1,0:T(8,128)(2,1)} %param.8) | copy-start | bytes 3145732
  10.4 34.7 %collective-permute-start.1 = (bf16[512,512]{0,1:T(8,128)(2,1)}, bf16[512,512]{0,1:T(8,128)(2,1)}, u32[]{:S(2)}, u32[]{:S(2)}) collective-permute-start(bf16[512,512]{0,1:T(8,128)(2,1)} %slice.54), channel_id=1, source_target_pairs={{0,4},{4,8},{8,12},{12,16},{16,20},{20,24},{24,28},{28,32},{32,36}... | collective-permute-start | bytes 1572872 | tf_op jit(solution)/shard_map/ppermute | solution.py:16
  17.0 26.4 %collective-permute-start = (bf16[512,512]{1,0:T(8,128)(2,1)}, bf16[512,512]{1,0:T(8,128)(2,1)}, u32[]{:S(2)}, u32[]{:S(2)}) collective-permute-start(bf16[512,512]{1,0:T(8,128)(2,1)} %slice.41), channel_id=1, source_target_pairs={{0,4},{4,8},{8,12},{12,16},{16,20},{20,24},{24,28},{28,32},{32,36}... | collective-permute-start | bytes 1572872 | tf_op jit(solution)/shard_map/ppermute | solution.py:16
  31.1 6.2 copy-start.5
  37.3 5.1 copy-start.3
  53.8 86.8 %copy-start.8 = (bf16[4,512,128]{1,2,0:T(8,128)(2,1)S(1)}, bf16[4,512,128]{1,2,0:T(8,128)(2,1)}, u32[]{:S(2)}) copy-start(bf16[4,512,128]{1,2,0:T(8,128)(2,1)} %fusion.32) | copy-start | bytes 1572868
  140.6 10.5 %copy-start.4 = (bf16[256,4096]{1,0:T(8,128)(2,1)S(1)}, bf16[256,4096]{1,0:T(8,128)(2,1)}, u32[]{:S(2)}) copy-start(bf16[256,4096]{1,0:T(8,128)(2,1)} %param.10) | copy-start | bytes 6291460
  586.1 5.8 copy-start
  591.9 2.4 copy-start.7
  621.4 45.2 %all-to-all-start = ((bf16[2,512,4,384]{3,2,0,1:T(4,128)(2,1)}), bf16[2,512,4,384]{3,2,0,1:T(4,128)(2,1)S(1)}, u32[]{:S(2)}, u32[]{:S(2)}) async-start(bf16[2,512,4,384]{3,2,0,1:T(4,128)(2,1)} %copy.49), calls=%async_computation | async-start | bytes 6291456 | tf_op jit(solution)/shard_map/all_to_all | solution.py:97
  683.8 20.5 %all-to-all-start.1 = ((bf16[64,16,4,128]{3,2,1,0:T(4,128)(2,1)}), bf16[64,16,4,128]{3,2,1,0:T(4,128)(2,1)S(1)}, u32[]{:S(2)}, u32[]{:S(2)}) async-start(bf16[64,16,4,128]{3,2,1,0:T(4,128)(2,1)} %copy.52), calls=%async_computation.1 | async-start | bytes 2097152 | tf_op jit(solution)/shard_map/all_to_all | solution.py:99
Sparse Core Ops, SparseCore 0:
  9.6 130.9 all-gather.2
  142.2 206.2 all-gather.4
where the time goes:
time: 716 us; the launch traced here: 713 us
  blocking collectives  430 us (60%)
  waiting for transfers between devices  134 us (19%)
  matrix products  51.9 us (7%)
  local copies, waits for them, and re-layouts  40.4 us (6%)
  other arithmetic  22.4 us (3%)
  starting transfers between devices  20 us (3%)
  between operations  14.2 us (2%)
    psum x1, blocking collectives, per_device(): stream_all = lax.psum(terms, 'head').astype(jnp.bfloat16)  430 us
    all_gather x1, waiting for transfers between devices, per_device(): full_out = lax.all_gather(out_weight, 'seq', axis=1, tiled=True)  82.5 us
    all_to_all x1, waiting for transfers between devices, per_device(): lax.all_to_all(column_qkv, 'seq', split_axis=1, concat_axis=0, tiled=True)  38.8 us
    dot_general x1, matrix products, per_device(): projected = jnp.dot(normed_all, flat, preferred_element_type=jnp.float32)  19.4 us
  transfers between devices with their start and end apart: 6, of which 3 were waited for; matrix products, arithmetic and copies ran while one was open for 9% of the time, Pallas kernels for 0%

commit v1 on v0

v1 whole, which is shorter than its diff:
```python
import functools

import jax
import jax.numpy as jnp
from jax import lax
from jax.experimental import pallas as pl
from jax.experimental.pallas import tpu as pltpu
from jax.sharding import PartitionSpec as P

HD = 128
COLS = 512
GROUPS = 4
MESH = pl.DeviceIdType.MESH
EPS = 1e-05
EXP2_SCALE = HD ** (-0.5) * 1.4426950408889634
BF16 = jnp.bfloat16
F32 = jnp.float32


def aligned(value, by):
    return pl.multiple_of(value, by)


def ring4(value):
    return lax.rem(value + 8, 4)


class Place:
    def __init__(self):
        self.s = lax.axis_index("seq")
        self.h = lax.axis_index("head")
        self.z_lo = lax.div(self.s, 16)
        self.yx = lax.rem(self.s, 16)
        self.y = lax.div(self.yx, 4)
        self.x = lax.rem(self.s, 4)
        self.z_hi = lax.div(self.h, 2)
        self.core = lax.rem(self.h, 2)
        self.z = self.z_hi * 2 + self.z_lo

    def device(self, z, y, x, core):
        return (lax.rem(z, 2) * 16 + y * 4 + x, lax.div(z, 2) * 2 + core)

    def first(self, half, d):
        if half == 0:
            return self.device(self.z, self.y, ring4(self.x + d), self.core)
        return self.device(self.z, ring4(self.y + d), self.x, self.core)

    def second(self, half, d):
        return self.first(1 - half, d)

    def block(self, half, df, ds):
        if half == 0:
            return ring4(self.y - ds), ring4(self.x - df)
        return ring4(self.y - df), ring4(self.x - ds)

    def sibling(self):
        return (self.s, self.z_hi * 2 + 1 - self.core)

    def at_z(self, d):
        return self.device(ring4(self.z + d), self.y, self.x, self.core)


def remote(src, dst, send, recv, device):
    return pltpu.make_async_remote_copy(
        src_ref=src, dst_ref=dst, send_sem=send, recv_sem=recv, device_id=device, device_id_type=MESH
    )


def greet(barrier, device):
    pl.semaphore_signal(barrier, inc=1, device_id=device, device_id_type=MESH)


def contract_last(a, b):
    return lax.dot_general(a, b, (((1,), (1,)), ((), ())), preferred_element_type=F32)


def dot(a, b):
    return jnp.dot(a, b, preferred_element_type=F32)


def band_head(queries, keys_prev, keys, values_prev, values, has_prev):
    n = queries.shape[0]
    row = lax.broadcasted_iota(jnp.int32, (n, n), 0)
    col = lax.broadcasted_iota(jnp.int32, (n, n), 1)
    here = col <= row
    back = contract_last(queries, keys_prev)
    back = jnp.where(has_prev, back, -jnp.inf)
    scores = jnp.where(here, contract_last(queries, keys), back)
    top = jnp.max(scores, -1, keepdims=True)
    weights = jnp.exp2((scores - top) * EXP2_SCALE)
    total = jnp.sum(weights, -1, keepdims=True)
    own = jnp.where(here, weights, 0.0).astype(BF16)
    prev = jnp.where(here, 0.0, weights).astype(BF16)
    result = dot(own, values) + dot(prev, values_prev)
    return (result / total).astype(BF16)


def front(
    q, k, v, res, wo, gain, res_out, normed,
    halo, rows, rows_in, w, part, part_in, acc,
    halo_s, halo_r, row_s, row_r, z_s, z_r, f_s, f_r, s_s, s_r, o_s, o_r, p_s, p_r,
):
    me = Place()
    here = (me.s, me.h)
    features = q.shape[1]
    depth = wo.shape[0]
    half_rows, quarter = depth // 2, depth // 4
    share = res.shape[0]
    chunk = 512
    chunks = res.shape[1] // chunk

    barrier = pltpu.get_barrier_semaphore()
    last = me.s == 31

    @pl.when(me.s > 0)
    def _():
        greet(barrier, (me.s - 1, me.h))

    for d in (1, 2, 3):
        greet(barrier, me.at_z(d))
        greet(barrier, me.first(0, d))
        greet(barrier, me.first(1, d))
    greet(barrier, me.sibling())

    @pl.when(last)
    def _():
        pl.semaphore_wait(barrier, 10)

    @pl.when(jnp.logical_not(last))
    def _():
        pl.semaphore_wait(barrier, 11)

    def halo_copy(which):
        source = (k, v)[which]
        return remote(
            source.at[pl.ds(COLS, COLS)], halo.at[which], halo_s.at[which], halo_r.at[which],
            (lax.rem(me.s + 1, 32), me.h),
        )

    @pl.when(jnp.logical_not(last))
    def _():
        halo_copy(0).start()
        halo_copy(1).start()

    @pl.when(me.s == 0)
    def _():
        halo[...] = jnp.zeros_like(halo)

    def slot(dz, half, df, ds, offset, count):
        zz = ring4(me.z - dz)
        yy, xx = me.block(half, df, ds)
        return w.at[
            pl.ds(aligned(lax.div(zz, 2) * depth + offset, 16), count),
            pl.ds(aligned((lax.rem(zz, 2) * 16 + yy * 4 + xx) * 128, 128), 128),
        ]

    def z_copy(d):
        spot = slot(0, 0, 0, 0, 0, depth)
        return remote(wo, spot, z_s.at[d - 1], z_r.at[d - 1], me.at_z(d))

    def z_land(d):
        spot = slot(d, 0, 0, 0, 0, depth)
        return remote(spot, spot, z_s.at[d - 1], z_r.at[d - 1], me.at_z(d))

    def f_copy(half, dz, d, landing=False):
        spot = slot(dz, half, d if landing else 0, 0, half * half_rows, half_rows)
        return remote(spot, spot, f_s.at[half, dz, d - 1], f_r.at[half, dz, d - 1], me.first(half, d))

    def s_copy(half, way, dz, df, landing=False):
        step = 1 - 2 * way
        spot = slot(dz, half, df, step if landing else 0, half * half_rows, half_rows)
        i = dz * 4 + df
        return remote(spot, spot, s_s.at[half, way, i], s_r.at[half, way, i], me.second(half, step))

    def o_copy(half, way, dz, df, landing=False):
        step = 1 - 2 * way
        spot = slot(dz, half, df, 2 * step if landing else step, half * half_rows + way * quarter, quarter)
        i = dz * 4 + df
        return remote(spot, spot, o_s.at[half, way, i], o_r.at[half, way, i], me.second(half, step))

    for d in (1, 2, 3):
        z_copy(d).start()
    w[
        pl.ds(aligned(me.z_hi * depth, 16), depth), pl.ds(aligned(me.s * 128, 128), 128)
    ] = wo[...]

    def spread(dz):
        for half in (0, 1):
            for d in (1, 3, 2):
                f_copy(half, dz, d).start()
        for half in (0, 1):
            for way in (0, 1):
                s_copy(half, way, dz, 0).start()

    spread(0)

    def attend(line, keys_prev, values_prev, has_prev):
        top = line * COLS
        for g in range(GROUPS):
            cols = slice(g * HD, (g + 1) * HD)
            rows[line, :, cols] = band_head(
                q[top : top + COLS, cols],
                keys_prev[:, cols],
                k[top : top + COLS, cols],
                values_prev[:, cols],
                v[top : top + COLS, cols],
                has_prev,
            )

    def row_copy():
        return remote(rows.at[1 - me.z_hi], rows_in, row_s.at[0], row_r.at[0], me.at_z(2))

    attend(1, k.at[pl.ds(0, COLS)], v.at[pl.ds(0, COLS)], True)

    @pl.when(me.z_hi == 0)
    def _():
        row_copy().start()

    @pl.loop(1, 4)
    def _(dz):
        z_land(dz).wait_recv()
        spread(dz)

    @pl.loop(0, 4)
    def _(dz):
        for df in (1, 3, 2):
            for half in (0, 1):
                f_copy(half, dz, df, True).wait_recv()
                for way in (0, 1):
                    s_copy(half, way, dz, df).start()

    @pl.when(me.s > 0)
    def _():
        halo_copy(0).wait_recv()
        halo_copy(1).wait_recv()

    attend(0, halo.at[0], halo.at[1], me.s > 0)

    @pl.when(me.z_hi == 1)
    def _():
        row_copy().start()

    @pl.loop(0, 4)
    def _(dz):
        for df in range(4):
            for half in (0, 1):
                for way in (0, 1):
                    s_copy(half, way, dz, df, True).wait_recv()
                    o_copy(half, way, dz, df).start()

    @pl.loop(0, 4)
    def _(dz):
        for df in range(4):
            for half in (0, 1):
                for way in (0, 1):
                    o_copy(half, way, dz, df, True).wait_recv()

    row_copy().wait_recv()

    def product(of_core, columns):
        mine = pl.ds(aligned(of_core * share, 16), share)
        kept = dot(rows[me.z_hi, mine, :], w[pl.ds(aligned(me.z_hi * depth, 16), depth), columns])
        came = dot(rows_in[mine, :], w[pl.ds(aligned((1 - me.z_hi) * depth, 16), depth), columns])
        return kept + came

    def p_copy(n):
        columns = pl.ds(aligned(n * chunk, chunk), chunk)
        return remote(part.at[:, columns], part_in.at[:, columns], p_s.at[n], p_r.at[n], me.sibling())

    @pl.loop(0, chunks)
    def _(n):
        columns = pl.ds(aligned(n * chunk, chunk), chunk)
        part[:, columns] = product(1 - me.core, columns)
        p_copy(n).start()
        acc[:, columns] = product(me.core, columns) + res[:, columns].astype(F32)

    def settle(n, total):
        columns = pl.ds(aligned(n * chunk, chunk), chunk)
        p_copy(n).wait_recv()
        value = (acc[:, columns] + part_in[:, columns]).astype(BF16)
        res_out[:, columns] = value
        return total + jnp.sum(value.astype(F32), -1, keepdims=True)

    total = lax.fori_loop(0, chunks, settle, jnp.zeros((share, 1), F32))
    width = res.shape[1]
    mean = total / width

    def spread_of(n, total):
        columns = pl.ds(aligned(n * chunk, chunk), chunk)
        center = res_out[:, columns].astype(F32) - mean
        return total + jnp.sum(center * center, -1, keepdims=True)

    variance = lax.fori_loop(0, chunks, spread_of, jnp.zeros((share, 1), F32)) / width
    scale = lax.rsqrt(variance + EPS)

    @pl.loop(0, chunks)
    def _(n):
        columns = pl.ds(aligned(n * chunk, chunk), chunk)
        center = res_out[:, columns].astype(F32) - mean
        normed[:, columns] = (center * scale * gain[:, columns]).astype(BF16)

    @pl.when(jnp.logical_not(last))
    def _():
        halo_copy(0).wait_send()
        halo_copy(1).wait_send()

    row_copy().wait_send()
    for d in (1, 2, 3):
        z_copy(d).wait_send()

    @pl.loop(0, 4)
    def _(dz):
        for half in (0, 1):
            for d in (1, 2, 3):
                f_copy(half, dz, d).wait_send()
            for way in (0, 1):
                for df in range(4):
                    s_copy(half, way, dz, df).wait_send()
                    o_copy(half, way, dz, df).wait_send()

    @pl.loop(0, chunks)
    def _(n):
        p_copy(n).wait_send()


def back(
    normed, wq, out, n_buf, w, qkv, att, ship,
    e_s, e_r, f_s, f_r, s_s, s_r, o_s, o_r, b_s, b_r,
    n_s, n_r, zn_s, zn_r, zo_s, zo_r, out_s, out_r, own_sem,
):
    me = Place()
    depth = wq.shape[0]
    half_rows, quarter = depth // 2, depth // 4
    width = normed.shape[1]
    stays = me.z_lo == me.core
    line = 16

    barrier = pltpu.get_barrier_semaphore()

    def in_plane(d):
        spot = lax.rem(me.yx + d + 32, 16)
        return me.device(me.z, lax.div(spot, 4), lax.rem(spot, 4), me.core)

    for d in range(1, 16):
        greet(barrier, in_plane(d))
    greet(barrier, me.at_z(1))
    greet(barrier, me.at_z(3))
    greet(barrier, me.sibling())

    swap = (me.core * 16 + me.yx, me.z_hi * 2 + me.z_lo)

    @pl.when(jnp.logical_not(stays))
    def _():
        greet(barrier, swap)

    def source(d):
        spot = lax.rem(me.yx + lax.rem(d, 16), 16)
        core = lax.rem(me.core + lax.div(d, 16), 2)
        return me.device(me.h, lax.div(spot, 4), lax.rem(spot, 4), core)

    @pl.loop(1, 32)
    def _(d):
        greet(barrier, source(d))

    @pl.when(jnp.logical_not(stays))
    def _():
        greet(barrier, source(0))

    @pl.when(stays)
    def _():
        pl.semaphore_wait(barrier, 15 + 3 + 31)

    @pl.when(jnp.logical_not(stays))
    def _():
        pl.semaphore_wait(barrier, 15 + 3 + 1 + 32)

    def slot(core, half, df, ds, offset, count):
        yy, xx = me.block(half, df, ds)
        return w.at[pl.ds(aligned((core * 16 + yy * 4 + xx) * depth + offset, 16), count)]

    def swap_copy():
        return remote(
            wq, w.at[pl.ds(aligned(me.s * depth, 16), depth)], e_s.at[0], e_r.at[0], swap
        )

    def swap_land():
        spot = slot(me.core, 0, 0, 0, 0, depth)
        return remote(spot, spot, e_s.at[0], e_r.at[0], swap)

    @pl.when(jnp.logical_not(stays))
    def _():
        swap_copy().start()

    def n_spot(dz, d):
        rows = pl.ds(aligned(lax.rem(me.yx - d + 32, 16) * line, line), line)
        return n_buf.at[ring4(me.z - dz), rows]

    def n_copy(d, landing=False):
        if landing:
            spot = n_spot(0, d)
            return remote(spot, spot, n_s.at[d], n_r.at[d], in_plane(d))
        src = normed.at[pl.ds(aligned(lax.rem(me.yx + d, 16) * line, line), line)]
        return remote(src, n_spot(0, 0), n_s.at[d], n_r.at[d], in_plane(d))

    def zn_copy(way, d, landing=False):
        step = 1 - 2 * way
        spot = n_spot(step if landing else 0, d)
        return remote(spot, spot, zn_s.at[way, d], zn_r.at[way, d], me.at_z(step))

    def zo_copy(way, d, landing=False):
        step = 1 - 2 * way
        spot = n_spot(2 * step if landing else step, d).at[:, pl.ds(way * (width // 2), width // 2)]
        return remote(spot, spot, zo_s.at[way, d], zo_r.at[way, d], me.at_z(step))

    n_buf[me.z, pl.ds(aligned(me.yx * line, line), line), :] = normed[
        pl.ds(aligned(me.yx * line, line), line), :
    ]
    for way in (0, 1):
        zn_copy(way, 0).start()

    @pl.loop(1, 16)
    def _(d):
        n_copy(d).start()

    @pl.when(stays)
    def _():
        w[pl.ds(aligned(me.s * depth, 16), depth), :] = wq[...]

    @pl.when(jnp.logical_not(stays))
    def _():
        swap_land().wait_recv()

    def f_copy(half, d, landing=False):
        spot = slot(me.core, half, d if landing else 0, 0, half * half_rows, half_rows)
        return remote(spot, spot, f_s.at[half, d - 1], f_r.at[half, d - 1], me.first(half, d))

    def s_copy(half, way, df, landing=False):
        step = 1 - 2 * way
        spot = slot(me.core, half, df, step if landing else 0, half * half_rows, half_rows)
        return remote(spot, spot, s_s.at[half, way, df], s_r.at[half, way, df], me.second(half, step))

    def o_copy(half, way, df, landing=False):
        step = 1 - 2 * way
        spot = slot(me.core, half, df, 2 * step if landing else step, half * half_rows + way * quarter, quarter)
        return remote(spot, spot, o_s.at[half, way, df], o_r.at[half, way, df], me.second(half, step))

    def b_copy(half, df, ds, landing=False):
        core = 1 - me.core if landing else me.core
        spot = slot(core, half, df, ds, half * half_rows, half_rows)
        i = df * 4 + ring4(ds)
        return remote(spot, spot, b_s.at[half, i], b_r.at[half, i], me.sibling())

    for half in (0, 1):
        for d in (1, 3, 2):
            f_copy(half, d).start()
    for half in (0, 1):
        for way in (0, 1):
            s_copy(half, way, 0).start()
        b_copy(half, 0, 0).start()

    @pl.loop(1, 16)
    def _(d):
        n_copy(d, True).wait_recv()
        for way in (0, 1):
            zn_copy(way, d).start()

    for df in (1, 3, 2):
        for half in (0, 1):
            f_copy(half, df, True).wait_recv()
            for way in (0, 1):
                s_copy(half, way, df).start()
            b_copy(half, df, 0).start()
    for df in (0, 1, 3, 2):
        for half in (0, 1):
            for way in (0, 1):
                s_copy(half, way, df, True).wait_recv()
                o_copy(half, way, df).start()
                b_copy(half, df, 1 - 2 * way).start()

    @pl.loop(0, 16)
    def _(d):
        for way in (0, 1):
            zn_copy(way, d, True).wait_recv()
            zo_copy(way, d).start()

    for df in (0, 1, 3, 2):
        for half in (0, 1):
            for way in (0, 1):
                o_copy(half, way, df, True).wait_recv()
            b_copy(half, df, 2).start()

    for half in (0, 1):
        for df in range(4):
            for ds in range(4):
                b_copy(half, df, ds, True).wait_recv()

    size = line * 16
    at = lax.broadcasted_iota(jnp.int32, (size, size), 0)
    to = lax.broadcasted_iota(jnp.int32, (size, size), 1)
    turn = (to == (at & 15) * 16 + (at >> 4)).astype(F32).astype(BF16)
    chunk = 512

    def project(dz):
        zz = ring4(me.z - dz)

        @pl.loop(0, w.shape[1] // chunk)
        def _(n):
            columns = pl.ds(aligned(n * chunk, chunk), chunk)
            value = dot(n_buf[zz], w[:, columns]).astype(BF16)
            turned = dot(turn, value).astype(BF16)
            qkv[:, pl.ds(aligned(zz * 16, 16), 16), columns] = turned.reshape(16, 16, chunk)

    project(0)
    project(1)
    project(3)

    @pl.loop(0, 16)
    def _(d):
        for way in (0, 1):
            zo_copy(way, d, True).wait_recv()

    project(2)

    grid_row = 2 * (((at >> 4) & 1) * 16 + (at & 15)) + ((at >> 5) & 1)
    grid_row_k = 2 * (((to >> 4) & 1) * 16 + (to & 15)) + ((to >> 5) & 1)
    allowed = ((at >> 6) == (to >> 6)) & (grid_row_k <= grid_row)

    @pl.loop(0, 4)
    def _(block):
        columns = pl.ds(block * 4, 4)
        for g in range(GROUPS):
            base = g * 3 * HD
            queries = qkv[columns, :, base : base + HD].reshape(size, HD)
            keys = qkv[columns, :, base + HD : base + 2 * HD].reshape(size, HD)
            values = qkv[columns, :, base + 2 * HD : base + 3 * HD].reshape(size, HD)
            scores = jnp.where(allowed, contract_last(queries, keys), -jnp.inf)
            top = jnp.max(scores, -1, keepdims=True)
            weights = jnp.exp2((scores - top) * EXP2_SCALE)
            total = jnp.sum(weights, -1, keepdims=True)
            result = (dot(weights.astype(BF16), values) / total).astype(BF16)
            att[columns, :, g * HD : (g + 1) * HD] = result.reshape(4, 64, HD)

    for zz in range(4):
        plane = att[:, zz * 16 : (zz + 1) * 16, :].reshape(size, GROUPS * HD)
        ship[zz // 2, zz % 2] = dot(turn, plane).astype(BF16)

    mine = pl.ds(aligned(me.core * 256 + me.yx * line, line), line)

    def out_copy(d):
        spot = lax.rem(me.yx - lax.rem(d, 16) + 16, 16)
        z_lo = lax.rem(me.z_lo + lax.div(d, 16), 2)
        src = ship.at[:, z_lo, pl.ds(aligned(spot * line, line), line)]
        i = lax.rem(d, 16) + 16 * lax.rem(me.core + me.z_lo, 2)
        return remote(src, out.at[:, mine], out_s.at[d], out_r.at[i], (z_lo * 16 + spot, me.z))

    def out_land(d):
        spot = lax.rem(me.yx + lax.rem(d, 16), 16)
        core = lax.rem(me.core + lax.div(d, 16), 2)
        dst = out.at[:, pl.ds(aligned(core * 256 + spot * line, line), line)]
        return remote(dst, dst, out_s.at[d], out_r.at[d], source(d))

    own = pltpu.make_async_copy(
        ship.at[:, me.z_lo, pl.ds(aligned(me.yx * line, line), line)], out.at[:, mine], own_sem.at[0]
    )

    @pl.loop(1, 32)
    def _(d):
        out_copy(d).start()

    @pl.when(stays)
    def _():
        own.start()

    @pl.when(jnp.logical_not(stays))
    def _():
        out_copy(0).start()

    @pl.loop(1, 32)
    def _(d):
        out_land(d).wait_recv()

    @pl.when(stays)
    def _():
        own.wait()

    @pl.when(jnp.logical_not(stays))
    def _():
        out_land(0).wait_recv()
        out_copy(0).wait_send()
        swap_copy().wait_send()

    @pl.loop(1, 32)
    def _(d):
        out_copy(d).wait_send()

    @pl.loop(1, 16)
    def _(d):
        n_copy(d).wait_send()

    @pl.loop(0, 16)
    def _(d):
        for way in (0, 1):
            zn_copy(way, d).wait_send()
            zo_copy(way, d).wait_send()

    for half in (0, 1):
        for d in (1, 2, 3):
            f_copy(half, d).wait_send()
        for df in range(4):
            for way in (0, 1):
                s_copy(half, way, df).wait_send()
                o_copy(half, way, df).wait_send()
            for ds in range(4):
                b_copy(half, df, ds).wait_send()


def in_vmem(count):
    return [pl.BlockSpec(memory_space=pltpu.VMEM)] * count


def per_device(row_queries, row_keys, row_values, residual_in, out_weight, norm_gain, qkv_weight):
    positions, features = row_queries.shape
    share, width = residual_in.shape
    depth = out_weight.shape[0]
    dma = pltpu.SemaphoreType.DMA
    residual_out, normed = pl.pallas_call(
        front,
        out_shape=(
            jax.ShapeDtypeStruct((share, width), BF16),
            jax.ShapeDtypeStruct((share, width), BF16),
        ),
        in_specs=in_vmem(6),
        out_specs=tuple(in_vmem(2)),
        scratch_shapes=[
            pltpu.VMEM((2, COLS, features), BF16),
            pltpu.VMEM((2, COLS, features), BF16),
            pltpu.VMEM((COLS, features), BF16),
            pltpu.VMEM((2 * depth, width), BF16),
            pltpu.VMEM((share, width), F32),
            pltpu.VMEM((share, width), F32),
            pltpu.VMEM((share, width), F32),
            dma((2,)), dma((2,)),
            dma((1,)), dma((1,)),
            dma((3,)), dma((3,)),
            dma((2, 4, 3)), dma((2, 4, 3)),
            dma((2, 2, 16)), dma((2, 2, 16)),
            dma((2, 2, 16)), dma((2, 2, 16)),
            dma((8,)), dma((8,)),
        ],
        compiler_params=pltpu.CompilerParams(
            collective_id=0, has_side_effects=True, vmem_limit_bytes=56 * 2**20
        ),
        name="front",
    )(row_queries, row_keys, row_values, residual_in, out_weight, norm_gain.reshape(1, -1))
    flat = qkv_weight.reshape(qkv_weight.shape[0], -1)
    columns = flat.shape[1]
    column_out = pl.pallas_call(
        back,
        out_shape=jax.ShapeDtypeStruct((2, COLS, features), BF16),
        in_specs=in_vmem(2),
        out_specs=in_vmem(1)[0],
        scratch_shapes=[
            pltpu.VMEM((4, 256, width), BF16),
            pltpu.VMEM((width, columns), BF16),
            pltpu.VMEM((16, 64, columns), BF16),
            pltpu.VMEM((16, 64, features), BF16),
            pltpu.VMEM((2, 2, 256, features), BF16),
            dma((1,)), dma((1,)),
            dma((2, 3)), dma((2, 3)),
            dma((2, 2, 4)), dma((2, 2, 4)),
            dma((2, 2, 4)), dma((2, 2, 4)),
            dma((2, 16)), dma((2, 16)),
            dma((16,)), dma((16,)),
            dma((2, 16)), dma((2, 16)),
            dma((2, 16)), dma((2, 16)),
            dma((32,)), dma((32,)),
            dma((1,)),
        ],
        compiler_params=pltpu.CompilerParams(
            collective_id=1, has_side_effects=True, vmem_limit_bytes=56 * 2**20
        ),
        name="back",
    )(normed, flat)
    return residual_out, column_out.reshape(positions, features)


def solution(mesh):
    placed = (
        P("seq", "head"),
        P("seq", "head"),
        P("seq", "head"),
        P(("seq", "head"), None),
        P("head", "seq"),
        P(),
        P("seq", "head", None, None),
    )
    return jax.shard_map(
        per_device,
        mesh=mesh,
        in_specs=placed,
        out_specs=(P(("seq", "head"), None), P("seq", "head")),
        check_vma=False,
    )
```

time: 716 us -> 216 us (0.30)
  blocking collectives: 430 us -> 0 us
  Pallas kernels: 0 us -> 211 us
  waiting for transfers between devices: 134 us -> 0 us
  matrix products: 51.9 us -> 0 us
  local copies, waits for them, and re-layouts: 40.4 us -> 4.13 us
  other arithmetic: 22.4 us -> 0 us
  starting transfers between devices: 20 us -> 0 us
  between operations: 14.2 us -> 0.7 us
    psum x1 -> x0, blocking collectives: 430 us -> none  [per_device(): stream_all = lax.psum(terms, 'head').astype(jnp.bfloat16)]
    pallas_call x0 -> x2, Pallas kernels: none -> 211 us  [the longest x1 116 us: per_device(): pl.pallas_call(back, out_shape=jax.ShapeDtypeStruct((2, COLS, features),...]
    all_gather x2 -> x0, waiting for transfers between devices: 82.6 us -> none  [the longest x1 82.5 us: per_device(): full_out = lax.all_gather(out_weight, 'seq', axis=1, tiled=True)]
    all_to_all x2 -> x0, waiting for transfers between devices: 50.4 us -> none  [the longest x1 38.8 us: per_device(): lax.all_to_all(column_qkv, 'seq', split_axis=1, concat_axis=0, tiled=True)]
    dot_general x6 -> x0, matrix products: 43.5 us -> none  [the longest x1 19.4 us: per_device(): projected = jnp.dot(normed_all, flat, preferred_element_type=jnp.float32)]
    all_to_all x2 -> x0, starting transfers between devices: 12 us -> none  [the longest x1 6.33 us: per_device(): lax.all_to_all(column_qkv, 'seq', split_axis=1, concat_axis=0, tiled=True)]
    all_to_all x3 -> x0, local copies, waits for them, and re-layouts: 11.8 us -> none  [the longest x2 11.3 us: per_device(): lax.all_to_all(column_qkv, 'seq', split_axis=1, concat_axis=0, tiled=True)]
    sub x2 -> x0, matrix products: 8.47 us -> none  [the longest x1 7.61 us: band_block(): shifted = jnp.exp(scores - jnp.max(scores, -1, keepdims=True))]
  transfers between devices with their start and end apart: 6 -> 0, of which waited for: 3 -> 0; matrix products, arithmetic and copies ran while one was open for 9% -> 0% of each run, Pallas kernels for 0% -> 0%
where the time goes in v1:
time: 216 us
  Pallas kernels  211 us (98%)
  local copies, waits for them, and re-layouts  4.13 us (2%)
    pallas_call x1, Pallas kernels, per_device(): pl.pallas_call(back, out_shape=jax.ShapeDtypeStruct((2, COLS, features),...  116 us
    pallas_call x1, Pallas kernels, per_device(): pl.pallas_call(front, out_shape=(jax.ShapeDtypeStruct((share, width), BF1...  94.5 us

profile of v1, /device:TPU:1, one launch (start us, length us, event | category | flops | bytes accessed | tf_op | source)
XLA Modules:
  0.0 215.7 jit_solution(3376145674729440993)
XLA Ops:
  0.6 0.0 copy-start.2
  0.6 94.5 %front.1 = (bf16[256,4096]{1,0:T(8,128)(2,1)}, bf16[256,4096]{1,0:T(8,128)(2,1)}) custom-call(bf16[1024,512]{1,0:T(8,128)(2,1)} %q.1, bf16[1024,512]{1,0:T(8,128)(2,1)} %k.1, bf16[1024,512]{1,0:T(8,128)(2,1)} %v.1, bf16[256,4096]{1,0:T(8,128)(2,1)} %res.1, bf16[512,128]{1,0:T(8,128)(2,1)} %wo.1, f32[1,4096]{1,0:T(1,128)} %bitcast.5), custom_call_target="tpu_custom_call" | custom-call | tf_op jit(solution)/shard_map/front/pallas_call | solution.py:626
  95.2 0.0 copy-done.2
  95.2 0.3 copy.10
  95.5 0.0 copy-start.1
  95.5 0.9 copy.11.wq
  96.4 116.3 %back.1 = bf16[2,512,512]{2,1,0:T(8,128)(2,1)} custom-call(bf16[256,4096]{1,0:T(8,128)(2,1)} %get-tuple-element.5.normed, bf16[128,1536]{1,0:T(8,128)(2,1)} %copy.11.wq), custom_call_target="tpu_custom_call" | custom-call | tf_op jit(solution)/shard_map/back/pallas_call | solution.py:657
  212.8 0.0 copy-done.1
  212.8 0.0 copy-start
  212.8 1.3 copy.14
  214.1 0.6 copy-done
  214.7 1.0 copy.15
Async XLA Ops:
  0.6 94.6 %copy-start.2 = (bf16[128,4,3,128]{3,1,2,0:T(4,128)(2,1)S(1)}, bf16[128,4,3,128]{3,1,2,0:T(4,128)(2,1)}, u32[]{:S(2)}) copy-start(bf16[128,4,3,128]{3,1,2,0:T(4,128)(2,1)} %param.13) | copy-start | bytes 1179652
  95.5 117.3 %copy-start.1 = (bf16[256,4096]{1,0:T(8,128)(2,1)S(1)}, bf16[256,4096]{1,0:T(8,128)(2,1)}, u32[]{:S(2)}) copy-start(bf16[256,4096]{1,0:T(8,128)(2,1)} %get-tuple-element.8) | copy-start | bytes 6291460
  212.8 1.9 copy-start

commit v2 on v0

v2 whole, which is shorter than its diff:
```python
import functools

import jax
import jax.numpy as jnp
from jax import lax
from jax.experimental import pallas as pl
from jax.experimental.pallas import tpu as pltpu
from jax.sharding import PartitionSpec as P

HD = 128
COLS = 512
GROUPS = 4
MESH = pl.DeviceIdType.MESH
EPS = 1e-05
EXP2_SCALE = HD ** (-0.5) * 1.4426950408889634
BF16 = jnp.bfloat16
F32 = jnp.float32


def aligned(value, by):
    return pl.multiple_of(value, by)


def ring4(value):
    return lax.rem(value + 8, 4)


class Place:
    def __init__(self):
        self.s = lax.axis_index("seq")
        self.h = lax.axis_index("head")
        self.z_lo = lax.div(self.s, 16)
        self.yx = lax.rem(self.s, 16)
        self.y = lax.div(self.yx, 4)
        self.x = lax.rem(self.s, 4)
        self.z_hi = lax.div(self.h, 2)
        self.core = lax.rem(self.h, 2)
        self.z = self.z_hi * 2 + self.z_lo

    def device(self, z, y, x, core):
        return (lax.rem(z, 2) * 16 + y * 4 + x, lax.div(z, 2) * 2 + core)

    def first(self, half, d):
        if half == 0:
            return self.device(self.z, self.y, ring4(self.x + d), self.core)
        return self.device(self.z, ring4(self.y + d), self.x, self.core)

    def second(self, half, d):
        return self.first(1 - half, d)

    def block(self, half, df, ds):
        if half == 0:
            return ring4(self.y - ds), ring4(self.x - df)
        return ring4(self.y - df), ring4(self.x - ds)

    def shifted(self, axis, d):
        z = ring4(self.z + d) if axis == "z" else self.z
        y = ring4(self.y + d) if axis == "y" else self.y
        x = ring4(self.x + d) if axis == "x" else self.x
        return self.device(z, y, x, self.core)

    def sibling(self):
        return (self.s, self.z_hi * 2 + 1 - self.core)

    def at_z(self, d):
        return self.device(ring4(self.z + d), self.y, self.x, self.core)


def remote(src, dst, send, recv, device):
    return pltpu.make_async_remote_copy(
        src_ref=src, dst_ref=dst, send_sem=send, recv_sem=recv, device_id=device, device_id_type=MESH
    )


def greet(barrier, device):
    pl.semaphore_signal(barrier, inc=1, device_id=device, device_id_type=MESH)


def contract_last(a, b):
    return lax.dot_general(a, b, (((1,), (1,)), ((), ())), preferred_element_type=F32)


def dot(a, b):
    return jnp.dot(a, b, preferred_element_type=F32)


def band_head(queries, keys_prev, keys, values_prev, values, has_prev):
    n = queries.shape[0]
    row = lax.broadcasted_iota(jnp.int32, (n, n), 0)
    col = lax.broadcasted_iota(jnp.int32, (n, n), 1)
    here = col <= row
    back = contract_last(queries, keys_prev)
    back = jnp.where(has_prev, back, -jnp.inf)
    scores = jnp.where(here, contract_last(queries, keys), back)
    top = jnp.max(scores, -1, keepdims=True)
    weights = jnp.exp2((scores - top) * EXP2_SCALE)
    total = jnp.sum(weights, -1, keepdims=True)
    own = jnp.where(here, weights, 0.0).astype(BF16)
    prev = jnp.where(here, 0.0, weights).astype(BF16)
    result = dot(own, values) + dot(prev, values_prev)
    return (result / total).astype(BF16)


PARTS = (
    (0, 192, ("z", "x", "y"), 96),
    (192, 128, ("z", "y", "x"), 0),
    (320, 192, ("x", "y", "z"), 96),
)
LINE = 16


def both(
    q_in, k_in, v_in, res_in, wo, gain, wq, res_hbm, out,
    q, k, v, res, res_out, normed, halo, rows, rows_in, w_out, part, part_in,
    n_buf, w, att, ship,
    in_sem, halo_s, halo_r, row_s, row_r, g1_s, g1_r, g2_s, g2_r, g3_s, g3_r, g4_s, g4_r, p_s, p_r,
    e_s, e_r, f_s, f_r, s_s, s_r, o_s, o_r, b_s, b_r,
    n_s, n_r, zn_s, zn_r, zo_s, zo_r, out_s, out_r,
):
    me = Place()
    here = (me.s, me.h)
    share, width = normed.shape
    depth = wo.shape[0]
    line = LINE
    chunk = 512
    chunks = width // chunk
    last = me.s == 31
    stays = me.z_lo == me.core
    moves = jnp.logical_not(stays)
    k_depth = wq.shape[0]
    half_rows, quarter = k_depth // 2, k_depth // 4

    own_block = w_out.at[
        pl.ds(aligned(me.z_hi * depth, 16), depth), pl.ds(aligned(me.s * 128, 128), 128)
    ]
    loads = [
        pltpu.make_async_copy(wo, own_block, in_sem.at[0]),
        pltpu.make_async_copy(k_in, k, in_sem.at[1]),
        pltpu.make_async_copy(q_in, q, in_sem.at[2]),
        pltpu.make_async_copy(v_in, v, in_sem.at[3]),
        pltpu.make_async_copy(res_in, res, in_sem.at[4]),
    ]
    for load in loads:
        load.start()
    own_rows = pltpu.make_async_copy(
        wq, w.at[pl.ds(aligned(me.s * k_depth, 16), k_depth)], in_sem.at[5]
    )

    @pl.when(stays)
    def _():
        own_rows.start()

    barrier = pltpu.get_barrier_semaphore()

    def landed(ref, sem):
        remote(ref, ref, sem, sem, me.sibling()).wait_recv()

    def gone(ref, sem):
        remote(ref, ref, sem, sem, me.sibling()).wait_send()

    def in_plane(d):
        spot = lax.rem(me.yx + d + 32, 16)
        return me.device(me.z, lax.div(spot, 4), lax.rem(spot, 4), me.core)

    swap = (me.core * 16 + me.yx, me.z_hi * 2 + me.z_lo)

    def source(d):
        spot = lax.rem(me.yx + lax.rem(d, 16), 16)
        core = lax.rem(me.core + lax.div(d, 16), 2)
        return me.device(me.h, lax.div(spot, 4), lax.rem(spot, 4), core)

    @pl.when(me.s > 0)
    def _():
        greet(barrier, (me.s - 1, me.h))

    @pl.loop(1, 16)
    def _(d):
        greet(barrier, in_plane(d))

    for d in (1, 2, 3):
        greet(barrier, me.at_z(d))
    greet(barrier, me.sibling())

    @pl.loop(1, 32)
    def _(d):
        greet(barrier, source(d))

    @pl.when(moves)
    def _():
        greet(barrier, swap)
        greet(barrier, source(0))

    moving = lax.rem(me.z_lo + me.core, 2)
    pl.semaphore_wait(barrier, 15 + 3 + 1 + 31 + 2 * moving + 1 - lax.div(me.s, 31))

    def halo_copy(i):
        which, piece = i // 8, i % 8
        return remote(
            (k_in, v_in)[which].at[8 + piece], halo.at[which, piece], halo_s.at[0], halo_r.at[0],
            (lax.rem(me.s + 1, 32), me.h),
        )

    def halo_start(pieces):
        @pl.when(jnp.logical_not(last))
        def _():
            for i in pieces:
                halo_copy(i).start()

    halo_start(range(2))

    @pl.when(me.s == 0)
    def _():
        halo[...] = jnp.zeros_like(halo)

    def spot_of(p, d1, d2, d3, offset, count):
        back_by = dict(zip(PARTS[p][2], (d1, d2, d3)))
        zz, yy, xx = ring4(me.z - back_by["z"]), ring4(me.y - back_by["y"]), ring4(me.x - back_by["x"])
        return w_out.at[
            pl.ds(aligned(lax.div(zz, 2) * depth + PARTS[p][0] + offset, 16), count),
            pl.ds(aligned((lax.rem(zz, 2) * 16 + yy * 4 + xx) * 128, 128), 128),
        ]

    def g1(p, d, landing=False):
        spot = spot_of(p, d if landing else 0, 0, 0, 0, PARTS[p][1])
        return remote(spot, spot, g1_s.at[p], g1_r.at[p, d - 1], me.shifted(PARTS[p][2][0], d))

    def g2(p, d1, d, landing=False):
        d2 = d if landing else (3 if d == 2 else 0)
        spot = spot_of(p, d1, d2, 0, 0, PARTS[p][1])
        to = me.shifted(PARTS[p][2][1], 3 if d == 2 else d)
        return remote(spot, spot, g2_s.at[p], g2_r.at[p, d1, d - 1], to)

    def g3(p, way, d1, d2, landing=False):
        step = 1 - 2 * way
        spot = spot_of(p, d1, d2, step if landing else 0, 0, PARTS[p][1])
        i = d1 * 4 + d2
        return remote(spot, spot, g3_s.at[p], g3_r.at[p, way, i], me.shifted(PARTS[p][2][2], step))

    def g4(p, way, d1, d2, landing=False):
        step = 1 - 2 * way
        plus = PARTS[p][3]
        offset, count = ((0, plus), (plus, PARTS[p][1] - plus))[way]
        spot = spot_of(p, d1, d2, 2 * step if landing else step, offset, count)
        return remote(spot, spot, g4_s.at[p], g4_r.at[p, way], me.shifted(PARTS[p][2][2], step))

    def far_ways(p):
        return (0, 1) if PARTS[p][3] else (1,)

    def send_on(p, d1, d2):
        for way in (0, 1):
            g3(p, way, d1, d2).start()

    loads[0].wait()
    for p in range(3):
        for d in (1, 3, 2):
            g1(p, d).start()
    for p in range(3):
        for d in (1, 3):
            g2(p, 0, d).start()
    for p in range(3):
        send_on(p, 0, 0)
        halo_start(range(2 + p, 3 + p))

    def swap_copy():
        return remote(
            wq, w.at[pl.ds(aligned(me.s * k_depth, 16), k_depth)], e_s.at[0], e_r.at[0], swap
        )

    @pl.when(moves)
    def _():
        swap_copy().start()

    def attend(top, prev_k, prev_v, prev_top, has_prev):
        for g in range(GROUPS):
            cols = slice(g * HD, (g + 1) * HD)

            def head_of(ref, start):
                return ref[start : start + 8, :, cols].reshape(COLS, HD)

            rows[top // 8, :, cols] = band_head(
                head_of(q, top), head_of(prev_k, prev_top), head_of(k, top),
                head_of(prev_v, prev_top), head_of(v, top), has_prev,
            )

    def row_copy():
        return remote(rows.at[1 - me.z_hi], rows_in, row_s.at[0], row_r.at[0], me.at_z(2))

    for load in loads[1:4]:
        load.wait()
    attend(8, k, v, 0, True)

    @pl.when(me.z_hi == 0)
    def _():
        row_copy().start()

    for d1 in range(1, 4):
        for p in range(3):
            g1(p, d1, True).wait_recv()
            for d in (1, 3):
                g2(p, d1, d).start()
            send_on(p, d1, 0)
        halo_start(range(2 + 3 * d1, 5 + 3 * d1))

    halo_start(range(14, 16))

    @pl.loop(0, 4)
    def _(d1):
        for p in range(3):
            g2(p, d1, 3, True).wait_recv()
            g2(p, d1, 2).start()
            send_on(p, d1, 3)
            g2(p, d1, 1, True).wait_recv()
            send_on(p, d1, 1)

    @pl.loop(0, 4)
    def _(d1):
        for p in range(3):
            g2(p, d1, 2, True).wait_recv()
            send_on(p, d1, 2)

    @pl.when(me.s > 0)
    def _():
        landed(halo, halo_r.at[0])

    attend(0, halo.at[0], halo.at[1], 0, me.s > 0)

    @pl.when(me.z_hi == 1)
    def _():
        row_copy().start()

    for d2 in (0, 3, 1, 2):

        @pl.loop(0, 4)
        def _(d1):
            for p in range(3):
                for way in (0, 1):
                    g3(p, way, d1, d2, True).wait_recv()
                    if way in far_ways(p):
                        g4(p, way, d1, d2).start()

    def slot(core, half, df, ds, offset, count):
        yy, xx = me.block(half, df, ds)
        return w.at[pl.ds(aligned((core * 16 + yy * 4 + xx) * k_depth + offset, 16), count)]

    def swap_land():
        spot = slot(me.core, 0, 0, 0, 0, k_depth)
        return remote(spot, spot, e_s.at[0], e_r.at[0], swap)

    def f_copy(half, d, landing=False):
        spot = slot(me.core, half, d if landing else 0, 0, half * half_rows, half_rows)
        return remote(spot, spot, f_s.at[0], f_r.at[half, d - 1], me.first(half, d))

    def s_copy(half, way, df, landing=False):
        step = 1 - 2 * way
        spot = slot(me.core, half, df, step if landing else 0, half * half_rows, half_rows)
        return remote(spot, spot, s_s.at[0], s_r.at[half, way, df], me.second(half, step))

    def o_copy(half, way, df, landing=False):
        step = 1 - 2 * way
        spot = slot(me.core, half, df, 2 * step if landing else step, half * half_rows + way * quarter, quarter)
        return remote(spot, spot, o_s.at[0], o_r.at[half, way, df], me.second(half, step))

    def b_copy(half, df, ds, landing=False):
        core = 1 - me.core if landing else me.core
        spot = slot(core, half, df, ds, half * half_rows, half_rows)
        return remote(spot, spot, b_s.at[0], b_r.at[0], me.sibling())

    @pl.when(stays)
    def _():
        own_rows.wait()

    @pl.when(moves)
    def _():
        swap_land().wait_recv()

    for half in (0, 1):
        for d in (1, 3, 2):
            f_copy(half, d).start()
    for half in (0, 1):
        for way in (0, 1):
            s_copy(half, way, 0).start()
        b_copy(half, 0, 0).start()

    for p in range(3):
        for way in far_ways(p):
            count = (PARTS[p][3], PARTS[p][1] - PARTS[p][3])[way]
            landed(w_out.at[pl.ds(0, count), pl.ds(0, width // 2)], g4_r.at[p, way])

    row_copy().wait_recv()

    def product(of_core, columns):
        mine = pl.ds(aligned(of_core * share, 16), share)
        kept = dot(rows[me.z_hi, mine, :], w_out[pl.ds(aligned(me.z_hi * depth, 16), depth), columns])
        came = dot(rows_in[mine, :], w_out[pl.ds(aligned((1 - me.z_hi) * depth, 16), depth), columns])
        return kept + came

    def p_copy(n):
        columns = pl.ds(aligned(n * chunk, chunk), chunk)
        return remote(part.at[:, columns], part_in.at[:, columns], p_s.at[0], p_r.at[n], me.sibling())

    @pl.loop(0, chunks)
    def _(n):
        columns = pl.ds(aligned(n * chunk, chunk), chunk)
        part[:, columns] = product(1 - me.core, columns)
        p_copy(n).start()

    loads[4].wait()

    def settle(n, total):
        columns = pl.ds(aligned(n * chunk, chunk), chunk)
        own = product(me.core, columns) + res[:, columns].astype(F32)
        p_copy(n).wait_recv()
        value = (own + part_in[:, columns]).astype(BF16)
        res_out[:, columns] = value
        return total + jnp.sum(value.astype(F32), -1, keepdims=True)

    mean = lax.fori_loop(0, chunks, settle, jnp.zeros((share, 1), F32)) / width
    res_copy = pltpu.make_async_copy(res_out, res_hbm, in_sem.at[6])
    res_copy.start()

    def spread_of(n, total):
        columns = pl.ds(aligned(n * chunk, chunk), chunk)
        center = res_out[:, columns].astype(F32) - mean
        return total + jnp.sum(center * center, -1, keepdims=True)

    variance = lax.fori_loop(0, chunks, spread_of, jnp.zeros((share, 1), F32)) / width
    scale = lax.rsqrt(variance + EPS)

    @pl.loop(0, chunks)
    def _(n):
        columns = pl.ds(aligned(n * chunk, chunk), chunk)
        center = res_out[:, columns].astype(F32) - mean
        normed[:, columns] = (center * scale * gain[:, columns]).astype(BF16)

    def n_spot(dz, d):
        rows = pl.ds(aligned(lax.rem(me.yx - d + 32, 16) * line, line), line)
        return n_buf.at[ring4(me.z - dz), rows]

    def n_copy(d, landing=False):
        if landing:
            spot = n_spot(0, d)
            return remote(spot, spot, n_s.at[0], n_r.at[d], in_plane(d))
        src = normed.at[pl.ds(aligned(lax.rem(me.yx + d, 16) * line, line), line)]
        return remote(src, n_spot(0, 0), n_s.at[0], n_r.at[d], in_plane(d))

    def zn_copy(way, d, landing=False):
        step = 1 - 2 * way
        spot = n_spot(step if landing else 0, d)
        return remote(spot, spot, zn_s.at[way], zn_r.at[way, d], me.at_z(step))

    def zo_copy(way, d, landing=False):
        step = 1 - 2 * way
        spot = n_spot(2 * step if landing else step, d).at[:, pl.ds(way * (width // 2), width // 2)]
        return remote(spot, spot, zo_s.at[way], zo_r.at[way], me.at_z(step))

    n_buf[me.z, pl.ds(aligned(me.yx * line, line), line), :] = normed[
        pl.ds(aligned(me.yx * line, line), line), :
    ]
    for way in (0, 1):
        zn_copy(way, 0).start()

    @pl.loop(1, 6)
    def _(d):
        n_copy(d).start()

    @pl.loop(1, 11)
    def _(d):
        n_copy(d, True).wait_recv()
        for way in (0, 1):
            zn_copy(way, d).start()
        n_copy(d + 5).start()

    @pl.loop(11, 16)
    def _(d):
        n_copy(d, True).wait_recv()
        for way in (0, 1):
            zn_copy(way, d).start()

    for df in (1, 3, 2):
        for half in (0, 1):
            f_copy(half, df, True).wait_recv()
            for way in (0, 1):
                s_copy(half, way, df).start()
            b_copy(half, df, 0).start()
    for df in (0, 1, 3, 2):
        for half in (0, 1):
            for way in (0, 1):
                s_copy(half, way, df, True).wait_recv()
                o_copy(half, way, df).start()
                b_copy(half, df, 1 - 2 * way).start()

    @pl.loop(0, 16)
    def _(d):
        for way in (0, 1):
            zn_copy(way, d, True).wait_recv()
            zo_copy(way, d).start()

    for df in (0, 1, 3, 2):
        for half in (0, 1):
            for way in (0, 1):
                o_copy(half, way, df, True).wait_recv()
            b_copy(half, df, 2).start()

    landed(w.at[pl.ds(0, width // 2)], b_r.at[0])

    size = line * 16
    at = lax.broadcasted_iota(jnp.int32, (size, size), 0)
    to = lax.broadcasted_iota(jnp.int32, (size, size), 1)
    turn = (to == (at & 15) * 16 + (at >> 4)).astype(F32).astype(BF16)
    wide = 6 * HD

    def project(dz):
        zz = ring4(me.z - dz)

        @pl.loop(0, 2)
        def _(n):
            value = dot(n_buf[zz], w[:, pl.ds(aligned(n * wide, wide), wide)]).astype(BF16)
            turned = dot(turn, value).astype(BF16)
            for j in range(2):
                for which, ref in enumerate((q, k, v)):
                    piece = turned[:, (3 * j + which) * HD : (3 * j + which + 1) * HD]
                    ref[
                        :, pl.ds(aligned(zz * 16, 16), 16), pl.ds(aligned((2 * n + j) * HD, HD), HD)
                    ] = piece.reshape(16, 16, HD)

    project(0)
    project(1)
    project(3)

    for way in (0, 1):
        landed(n_buf.at[0, :, pl.ds(0, width // 2)], zo_r.at[way])

    project(2)

    grid_row = 2 * (((at >> 4) & 1) * 16 + (at & 15)) + ((at >> 5) & 1)
    grid_row_k = 2 * (((to >> 4) & 1) * 16 + (to & 15)) + ((to >> 5) & 1)
    allowed = ((at >> 6) == (to >> 6)) & (grid_row_k <= grid_row)

    mine = pl.ds(aligned(me.core * 256 + me.yx * line, line), line)

    def head_columns(g):
        return pl.ds(aligned(g * HD, HD), HD)

    def out_copy(g, d):
        spot = lax.rem(me.yx - lax.rem(d, 16) + 16, 16)
        z_lo = lax.rem(me.z_lo + lax.div(d, 16), 2)
        src = ship.at[:, z_lo, pl.ds(aligned(spot * line, line), line), head_columns(g)]
        dst = out.at[:, mine, head_columns(g)]
        return remote(src, dst, out_s.at[g], out_r.at[g], (z_lo * 16 + spot, me.z))

    def own_copy(g):
        src = ship.at[:, me.z_lo, pl.ds(aligned(me.yx * line, line), line), head_columns(g)]
        return pltpu.make_async_copy(src, out.at[:, mine, head_columns(g)], out_r.at[g])

    @pl.loop(0, GROUPS)
    def _(g):
        cols = head_columns(g)
        for block in range(4):
            some = slice(4 * block, 4 * block + 4)
            queries = q[some, :, cols].reshape(size, HD)
            keys = k[some, :, cols].reshape(size, HD)
            values = v[some, :, cols].reshape(size, HD)
            scores = jnp.where(allowed, contract_last(queries, keys), -jnp.inf)
            top = jnp.max(scores, -1, keepdims=True)
            weights = jnp.exp2((scores - top) * EXP2_SCALE)
            total = jnp.sum(weights, -1, keepdims=True)
            result = (dot(weights.astype(BF16), values) / total).astype(BF16)
            att[some] = result.reshape(4, 64, HD)
        for zz in range(4):
            plane = att[:, zz * 16 : (zz + 1) * 16, :].reshape(size, HD)
            ship[zz // 2, zz % 2, :, cols] = dot(turn, plane).astype(BF16)

        @pl.when(stays)
        def _():
            own_copy(g).start()

        @pl.when(moves)
        def _():
            out_copy(g, 0).start()

        @pl.loop(1, 32)
        def _(d):
            out_copy(g, d).start()

    for g in range(GROUPS):
        landed(out.at[:, :, pl.ds(g * HD, HD)], out_r.at[g])

    @pl.when(stays)
    def _():
        for g in range(GROUPS):
            gone(rows.at[0, pl.ds(0, 31 * 16), pl.ds(0, 256)], out_s.at[g])

    @pl.when(moves)
    def _():
        for g in range(GROUPS):
            gone(rows.at[0, :, pl.ds(0, 256)], out_s.at[g])
        swap_copy().wait_send()

    gone(n_buf.at[0, pl.ds(0, 15 * line)], n_s.at[0])
    for way in (0, 1):
        gone(n_buf.at[0], zn_s.at[way])
        gone(n_buf.at[0, :, pl.ds(0, width // 2)], zo_s.at[way])
    gone(w.at[pl.ds(0, 6 * half_rows)], f_s.at[0])
    gone(w.at[pl.ds(0, 16 * half_rows)], s_s.at[0])
    gone(w.at[pl.ds(0, 16 * quarter)], o_s.at[0])
    gone(w.at[pl.ds(0, 32 * half_rows)], b_s.at[0])
    res_copy.wait()

    @pl.when(jnp.logical_not(last))
    def _():
        gone(halo, halo_s.at[0])

    row_copy().wait_send()
    for p in range(3):
        some = pl.ds(0, PARTS[p][1])
        gone(w_out.at[some, pl.ds(0, 3 * 128)], g1_s.at[p])
        gone(w_out.at[some, pl.ds(0, 12 * 128)], g2_s.at[p])
        gone(w_out.at[some], g3_s.at[p])
        gone(w_out.at[some, pl.ds(0, 16 * 128)], g4_s.at[p])
    gone(part, p_s.at[0])


def per_device(row_queries, row_keys, row_values, residual_in, out_weight, norm_gain, qkv_weight):
    positions, features = row_queries.shape
    share, width = residual_in.shape
    depth = out_weight.shape[0]
    flat = qkv_weight.reshape(qkv_weight.shape[0], -1)
    columns = flat.shape[1]
    dma = pltpu.SemaphoreType.DMA
    anywhere = pl.BlockSpec(memory_space=pl.ANY)
    inside = pl.BlockSpec(memory_space=pltpu.VMEM)

    def folded(array):
        return array.reshape(16, 64, features)

    def pair(sent, received):
        received = received if isinstance(received, tuple) else (received,)
        return [dma((sent,)), dma(received)]

    residual_out, column_out = pl.pallas_call(
        both,
        out_shape=(
            jax.ShapeDtypeStruct((share, width), BF16),
            jax.ShapeDtypeStruct((2, COLS, features), BF16),
        ),
        in_specs=[anywhere] * 5 + [inside, anywhere],
        out_specs=(anywhere, anywhere),
        scratch_shapes=[
            pltpu.VMEM((16, 64, features), BF16),
            pltpu.VMEM((16, 64, features), BF16),
            pltpu.VMEM((16, 64, features), BF16),
            pltpu.VMEM((share, width), BF16),
            pltpu.VMEM((share, width), BF16),
            pltpu.VMEM((share, width), BF16),
            pltpu.VMEM((2, 8, 64, features), BF16),
            pltpu.VMEM((2, COLS, features), BF16),
            pltpu.VMEM((COLS, features), BF16),
            pltpu.VMEM((2 * depth, width), BF16),
            pltpu.VMEM((share, width), F32),
            pltpu.VMEM((share, width), F32),
            pltpu.VMEM((4, 256, width), BF16),
            pltpu.VMEM((width, columns), BF16),
            pltpu.VMEM((16, 64, HD), BF16),
            pltpu.VMEM((2, 2, 256, features), BF16),
            dma((7,)),
            *pair(1, 1), *pair(1, 1),
            *pair(3, (3, 3)), *pair(3, (3, 4, 3)), *pair(3, (3, 2, 16)), *pair(3, (3, 2)), *pair(1, 8),
            *pair(1, 1), *pair(1, (2, 3)), *pair(1, (2, 2, 4)), *pair(1, (2, 2, 4)), *pair(1, 1),
            *pair(1, 16), *pair(2, (2, 16)), *pair(2, 2), *pair(GROUPS, GROUPS),
        ],
        compiler_params=pltpu.CompilerParams(
            collective_id=0, has_side_effects=True, vmem_limit_bytes=60 * 2**20
        ),
        name="both",
    )(
        folded(row_queries), folded(row_keys), folded(row_values),
        residual_in, out_weight, norm_gain.reshape(1, -1), flat,
    )
    return residual_out, column_out.reshape(positions, features)


def solution(mesh):
    placed = (
        P("seq", "head"),
        P("seq", "head"),
        P("seq", "head"),
        P(("seq", "head"), None),
        P("head", "seq"),
        P(),
        P("seq", "head", None, None),
    )
    return jax.shard_map(
        per_device,
        mesh=mesh,
        in_specs=placed,
        out_specs=(P(("seq", "head"), None), P("seq", "head")),
        check_vma=False,
    )
```

time: 716 us -> 191 us (0.27)
  blocking collectives: 430 us -> 0 us
  Pallas kernels: 0 us -> 183 us
  waiting for transfers between devices: 134 us -> 0 us
  matrix products: 51.9 us -> 0 us
  local copies, waits for them, and re-layouts: 40.4 us -> 6.38 us
  other arithmetic: 22.4 us -> 0 us
  starting transfers between devices: 20 us -> 0 us
  between operations: 14.2 us -> 0.65 us
    psum x1 -> x0, blocking collectives: 430 us -> none  [per_device(): stream_all = lax.psum(terms, 'head').astype(jnp.bfloat16)]
    pallas_call x0 -> x1, Pallas kernels: none -> 183 us  [per_device(): pl.pallas_call(both, out_shape=(jax.ShapeDtypeStruct((share, width), BF16...]
    all_gather x2 -> x0, waiting for transfers between devices: 82.6 us -> none  [the longest x1 82.5 us: per_device(): full_out = lax.all_gather(out_weight, 'seq', axis=1, tiled=True)]
    all_to_all x2 -> x0, waiting for transfers between devices: 50.4 us -> none  [the longest x1 38.8 us: per_device(): lax.all_to_all(column_qkv, 'seq', split_axis=1, concat_axis=0, tiled=True)]
    dot_general x6 -> x0, matrix products: 43.5 us -> none  [the longest x1 19.4 us: per_device(): projected = jnp.dot(normed_all, flat, preferred_element_type=jnp.float32)]
    all_to_all x2 -> x0, starting transfers between devices: 12 us -> none  [the longest x1 6.33 us: per_device(): lax.all_to_all(column_qkv, 'seq', split_axis=1, concat_axis=0, tiled=True)]
    all_to_all x3 -> x0, local copies, waits for them, and re-layouts: 11.8 us -> none  [the longest x2 11.3 us: per_device(): lax.all_to_all(column_qkv, 'seq', split_axis=1, concat_axis=0, tiled=True)]
    sub x2 -> x0, matrix products: 8.47 us -> none  [the longest x1 7.61 us: band_block(): shifted = jnp.exp(scores - jnp.max(scores, -1, keepdims=True))]
  transfers between devices with their start and end apart: 6 -> 0, of which waited for: 3 -> 0; matrix products, arithmetic and copies ran while one was open for 9% -> 0% of each run, Pallas kernels for 0% -> 0%
where the time goes in v2:
time: 191 us; the launch traced here: 190 us
  Pallas kernels  183 us (96%)
  local copies, waits for them, and re-layouts  6.38 us (3%)
    pallas_call x1, Pallas kernels, per_device(): pl.pallas_call(both, out_shape=(jax.ShapeDtypeStruct((share, width), BF16...  183 us
    unnamed x5, local copies, waits for them, and re-layouts  5.45 us

profile of v2, /device:TPU:1, one launch (start us, length us, event | category | flops | bytes accessed | tf_op | source)
XLA Modules:
  0.0 189.8 jit_solution(9915295197064226911)
XLA Ops:
  0.6 1.3 copy.10
  1.9 0.9 copy.11.wq
  2.8 182.8 %both.1 = (bf16[256,4096]{1,0:T(8,128)(2,1)}, bf16[2,512,512]{2,1,0:T(8,128)(2,1)}) custom-call(bf16[16,64,512]{2,1,0:T(8,128)(2,1)} %bitcast.8, bf16[16,64,512]{2,1,0:T(8,128)(2,1)} %bitcast.9, bf16[16,64,512]{2,1,0:T(8,128)(2,1)} %bitcast.10, bf16[256,4096]{1,0:T(8,128)(2,1)} %res_in.1, bf16[512,128]{1,0:T(8,128)(2,1)} %wo.1, f32[1,4096]{1,0:T(1,128)} %bitcast.11, ...), custom_call_target="tpu_custom_call" | custom-call | tf_op jit(solution)/shard_map/both/pallas_call | solution.py:640
  185.6 0.0 copy-start
  185.6 3.2 %copy.14 = bf16[256,4096]{1,0:T(8,128)(2,1)} copy(bf16[256,4096]{1,0:T(8,128)(2,1)} %get-tuple-element.8) | data formatting | bytes 4194304
  188.9 0.0 copy-done
  188.9 1.0 copy.15
Async XLA Ops:
  185.6 3.2 %copy-start = (bf16[2,512,512]{2,1,0:T(8,128)(2,1)S(1)}, bf16[2,512,512]{2,1,0:T(8,128)(2,1)}, u32[]{:S(2)}) copy-start(bf16[2,512,512]{2,1,0:T(8,128)(2,1)} %get-tuple-element.5) | copy-start | bytes 3145732

commit v3 on v2

--- a/solution.py
+++ b/solution.py
@@ -102,9 +102,9 @@
 
 
 PARTS = (
-    (0, 192, ("z", "x", "y"), 96),
-    (192, 128, ("z", "y", "x"), 0),
-    (320, 192, ("x", "y", "z"), 96),
+    (0, 224, ("z", "x", "y"), 112),
+    (224, 160, ("z", "y", "x"), 0),
+    (384, 128, ("x", "y", "z"), 64),
 )
 LINE = 16
 
@@ -112,7 +112,7 @@
 def both(
     q_in, k_in, v_in, res_in, wo, gain, wq, res_hbm, out,
     q, k, v, res, res_out, normed, halo, rows, rows_in, w_out, part, part_in,
-    n_buf, w, att, ship,
+    n_buf, w, att, ship, means, scales,
     in_sem, halo_s, halo_r, row_s, row_r, g1_s, g1_r, g2_s, g2_r, g3_s, g3_r, g4_s, g4_r, p_s, p_r,
     e_s, e_r, f_s, f_r, s_s, s_r, o_s, o_r, b_s, b_r,
     n_s, n_r, zn_s, zn_r, zo_s, zo_r, out_s, out_r,
@@ -193,11 +193,14 @@
     moving = lax.rem(me.z_lo + me.core, 2)
     pl.semaphore_wait(barrier, 15 + 3 + 1 + 31 + 2 * moving + 1 - lax.div(me.s, 31))
 
+    def head_slice(g):
+        return pl.ds(g * HD, HD)
+
     def halo_copy(i):
-        which, piece = i // 8, i % 8
+        which, cols = i % 2, head_slice(i // 2)
         return remote(
-            (k_in, v_in)[which].at[8 + piece], halo.at[which, piece], halo_s.at[0], halo_r.at[0],
-            (lax.rem(me.s + 1, 32), me.h),
+            (k_in, v_in)[which].at[pl.ds(8, 8), :, cols], halo.at[which, :, :, cols],
+            halo_s.at[0], halo_r.at[i], (lax.rem(me.s + 1, 32), me.h),
         )
 
     def halo_start(pieces):
@@ -259,7 +262,7 @@
             g2(p, 0, d).start()
     for p in range(3):
         send_on(p, 0, 0)
-        halo_start(range(2 + p, 3 + p))
+        halo_start((2 + p,))
 
     def swap_copy():
         return remote(
@@ -270,38 +273,53 @@
     def _():
         swap_copy().start()
 
-    def attend(top, prev_k, prev_v, prev_top, has_prev):
-        for g in range(GROUPS):
-            cols = slice(g * HD, (g + 1) * HD)
-
-            def head_of(ref, start):
-                return ref[start : start + 8, :, cols].reshape(COLS, HD)
-
-            rows[top // 8, :, cols] = band_head(
-                head_of(q, top), head_of(prev_k, prev_top), head_of(k, top),
-                head_of(prev_v, prev_top), head_of(v, top), has_prev,
-            )
-
-    def row_copy():
-        return remote(rows.at[1 - me.z_hi], rows_in, row_s.at[0], row_r.at[0], me.at_z(2))
+    def attend(top, prev_k, prev_v, has_prev, g):
+        cols = slice(g * HD, (g + 1) * HD)
+
+        def head_of(ref, start):
+            return ref[start : start + 8, :, cols].reshape(COLS, HD)
+
+        rows[top // 8, :, cols] = band_head(
+            head_of(q, top), head_of(prev_k, 0), head_of(k, top), head_of(prev_v, 0), head_of(v, top), has_prev
+        )
+
+    def row_copy(g):
+        cols = head_slice(g)
+        return remote(
+            rows.at[1 - me.z_hi, :, cols], rows_in.at[:, cols], row_s.at[0], row_r.at[0], me.at_z(2)
+        )
+
+    def second_row(g):
+        attend(8, k, v, True, g)
+
+        @pl.when(me.z_hi == 0)
+        def _():
+            row_copy(g).start()
+
+    def first_row(g):
+        @pl.when(me.s > 0)
+        def _():
+            for i in (2 * g, 2 * g + 1):
+                halo_copy(i).wait_recv()
+
+        attend(0, halo.at[0], halo.at[1], me.s > 0, g)
+
+        @pl.when(me.z_hi == 1)
+        def _():
+            row_copy(g).start()
 
     for load in loads[1:4]:
         load.wait()
-    attend(8, k, v, 0, True)
-
-    @pl.when(me.z_hi == 0)
-    def _():
-        row_copy().start()
-
+    second_row(0)
+    second_row(1)
     for d1 in range(1, 4):
         for p in range(3):
             g1(p, d1, True).wait_recv()
             for d in (1, 3):
                 g2(p, d1, d).start()
             send_on(p, d1, 0)
-        halo_start(range(2 + 3 * d1, 5 + 3 * d1))
-
-    halo_start(range(14, 16))
+        halo_start((4 + d1,))
+    second_row(2)
 
     @pl.loop(0, 4)
     def _(d1):
@@ -312,23 +330,16 @@
             g2(p, d1, 1, True).wait_recv()
             send_on(p, d1, 1)
 
+    second_row(3)
+
     @pl.loop(0, 4)
     def _(d1):
         for p in range(3):
             g2(p, d1, 2, True).wait_recv()
             send_on(p, d1, 2)
 
-    @pl.when(me.s > 0)
-    def _():
-        landed(halo, halo_r.at[0])
-
-    attend(0, halo.at[0], halo.at[1], 0, me.s > 0)
-
-    @pl.when(me.z_hi == 1)
-    def _():
-        row_copy().start()
-
-    for d2 in (0, 3, 1, 2):
+    for turn_at, d2 in enumerate((0, 3, 1, 2)):
+        first_row(turn_at)
 
         @pl.loop(0, 4)
         def _(d1):
@@ -386,7 +397,7 @@
             count = (PARTS[p][3], PARTS[p][1] - PARTS[p][3])[way]
             landed(w_out.at[pl.ds(0, count), pl.ds(0, width // 2)], g4_r.at[p, way])
 
-    row_copy().wait_recv()
+    landed(rows_in, row_r.at[0])
 
     def product(of_core, columns):
         mine = pl.ds(aligned(of_core * share, 16), share)
@@ -424,13 +435,13 @@
         return total + jnp.sum(center * center, -1, keepdims=True)
 
     variance = lax.fori_loop(0, chunks, spread_of, jnp.zeros((share, 1), F32)) / width
-    scale = lax.rsqrt(variance + EPS)
-
-    @pl.loop(0, chunks)
-    def _(n):
-        columns = pl.ds(aligned(n * chunk, chunk), chunk)
-        center = res_out[:, columns].astype(F32) - mean
-        normed[:, columns] = (center * scale * gain[:, columns]).astype(BF16)
+    means[...] = jnp.broadcast_to(mean, means.shape)
+    scales[...] = jnp.broadcast_to(lax.rsqrt(variance + EPS), scales.shape)
+
+    def normalize(d):
+        block = pl.ds(aligned(lax.rem(me.yx + d, 16) * line, line), line)
+        center = res_out[block, :].astype(F32) - means[block, 0:1]
+        normed[block, :] = (center * scales[block, 0:1] * gain[...]).astype(BF16)
 
     def n_spot(dz, d):
         rows = pl.ds(aligned(lax.rem(me.yx - d + 32, 16) * line, line), line)
@@ -453,24 +464,30 @@
         spot = n_spot(2 * step if landing else step, d).at[:, pl.ds(way * (width // 2), width // 2)]
         return remote(spot, spot, zo_s.at[way], zo_r.at[way], me.at_z(step))
 
+    normalize(0)
     n_buf[me.z, pl.ds(aligned(me.yx * line, line), line), :] = normed[
         pl.ds(aligned(me.yx * line, line), line), :
     ]
     for way in (0, 1):
         zn_copy(way, 0).start()
 
-    @pl.loop(1, 6)
+    @pl.loop(1, 10)
     def _(d):
+        normalize(d)
         n_copy(d).start()
 
-    @pl.loop(1, 11)
+    @pl.loop(10, 16)
+    def _(d):
+        normalize(d)
+
+    @pl.loop(1, 7)
     def _(d):
         n_copy(d, True).wait_recv()
         for way in (0, 1):
             zn_copy(way, d).start()
-        n_copy(d + 5).start()
-
-    @pl.loop(11, 16)
+        n_copy(d + 9).start()
+
+    @pl.loop(7, 16)
     def _(d):
         n_copy(d, True).wait_recv()
         for way in (0, 1):
@@ -509,19 +526,21 @@
     turn = (to == (at & 15) * 16 + (at >> 4)).astype(F32).astype(BF16)
     wide = 6 * HD
 
+    def project_pair(dz, n):
+        zz = ring4(me.z - dz)
+        value = dot(n_buf[zz], w[:, pl.ds(aligned(n * wide, wide), wide)]).astype(BF16)
+        turned = dot(turn, value).astype(BF16)
+        for j in range(2):
+            for which, ref in enumerate((q, k, v)):
+                piece = turned[:, (3 * j + which) * HD : (3 * j + which + 1) * HD]
+                ref[
+                    :, pl.ds(aligned(zz * 16, 16), 16), pl.ds(aligned((2 * n + j) * HD, HD), HD)
+                ] = piece.reshape(16, 16, HD)
+
     def project(dz):
-        zz = ring4(me.z - dz)
-
         @pl.loop(0, 2)
         def _(n):
-            value = dot(n_buf[zz], w[:, pl.ds(aligned(n * wide, wide), wide)]).astype(BF16)
-            turned = dot(turn, value).astype(BF16)
-            for j in range(2):
-                for which, ref in enumerate((q, k, v)):
-                    piece = turned[:, (3 * j + which) * HD : (3 * j + which + 1) * HD]
-                    ref[
-                        :, pl.ds(aligned(zz * 16, 16), 16), pl.ds(aligned((2 * n + j) * HD, HD), HD)
-                    ] = piece.reshape(16, 16, HD)
+            project_pair(dz, n)
 
     project(0)
     project(1)
@@ -529,8 +548,6 @@
 
     for way in (0, 1):
         landed(n_buf.at[0, :, pl.ds(0, width // 2)], zo_r.at[way])
-
-    project(2)
 
     grid_row = 2 * (((at >> 4) & 1) * 16 + (at & 15)) + ((at >> 5) & 1)
     grid_row_k = 2 * (((to >> 4) & 1) * 16 + (to & 15)) + ((to >> 5) & 1)
@@ -554,6 +571,10 @@
 
     @pl.loop(0, GROUPS)
     def _(g):
+        @pl.when(lax.rem(g, 2) == 0)
+        def _():
+            project_pair(2, lax.div(g, 2))
+
         cols = head_columns(g)
         for block in range(4):
             some = slice(4 * block, 4 * block + 4)
@@ -610,7 +631,7 @@
     def _():
         gone(halo, halo_s.at[0])
 
-    row_copy().wait_send()
+    gone(rows_in, row_s.at[0])
     for p in range(3):
         some = pl.ds(0, PARTS[p][1])
         gone(w_out.at[some, pl.ds(0, 3 * 128)], g1_s.at[p])
@@ -662,8 +683,10 @@
             pltpu.VMEM((width, columns), BF16),
             pltpu.VMEM((16, 64, HD), BF16),
             pltpu.VMEM((2, 2, 256, features), BF16),
+            pltpu.VMEM((share, 128), F32),
+            pltpu.VMEM((share, 128), F32),
             dma((7,)),
-            *pair(1, 1), *pair(1, 1),
+            *pair(1, 8), *pair(1, 1),
             *pair(3, (3, 3)), *pair(3, (3, 4, 3)), *pair(3, (3, 2, 16)), *pair(3, (3, 2)), *pair(1, 8),
             *pair(1, 1), *pair(1, (2, 3)), *pair(1, (2, 2, 4)), *pair(1, (2, 2, 4)), *pair(1, 1),
             *pair(1, 16), *pair(2, (2, 16)), *pair(2, 2), *pair(GROUPS, GROUPS),

time: 191 us -> 190 us (level)
  no operation moved by 1% of the time
where the time goes in v3:
time: 190 us; the launch traced here: 189 us
  Pallas kernels  182 us (96%)
  local copies, waits for them, and re-layouts  6.38 us (3%)
    pallas_call x1, Pallas kernels, per_device(): pl.pallas_call(both, out_shape=(jax.ShapeDtypeStruct((share, width), BF16...  182 us
    unnamed x5, local copies, waits for them, and re-layouts  5.45 us

profile of v3, /device:TPU:1, one launch (start us, length us, event | category | flops | bytes accessed | tf_op | source)
XLA Modules:
  0.0 188.8 jit_solution(16203734095359221721)
XLA Ops:
  0.6 1.3 copy.10
  1.9 0.9 copy.11.wq
  2.8 181.8 %both.1 = (bf16[256,4096]{1,0:T(8,128)(2,1)}, bf16[2,512,512]{2,1,0:T(8,128)(2,1)}) custom-call(bf16[16,64,512]{2,1,0:T(8,128)(2,1)} %bitcast.8, bf16[16,64,512]{2,1,0:T(8,128)(2,1)} %bitcast.9, bf16[16,64,512]{2,1,0:T(8,128)(2,1)} %bitcast.10, bf16[256,4096]{1,0:T(8,128)(2,1)} %res_in.1, bf16[512,128]{1,0:T(8,128)(2,1)} %wo.1, f32[1,4096]{1,0:T(1,128)} %bitcast.11, ...), custom_call_target="tpu_custom_call" | custom-call | tf_op jit(solution)/shard_map/both/pallas_call | solution.py:661
  184.6 0.0 copy-start
  184.6 3.2 %copy.14 = bf16[256,4096]{1,0:T(8,128)(2,1)} copy(bf16[256,4096]{1,0:T(8,128)(2,1)} %get-tuple-element.8) | data formatting | bytes 4194304
  187.8 0.0 copy-done
  187.8 1.0 copy.15
Async XLA Ops:
  184.6 3.2 %copy-start = (bf16[2,512,512]{2,1,0:T(8,128)(2,1)S(1)}, bf16[2,512,512]{2,1,0:T(8,128)(2,1)}, u32[]{:S(2)}) copy-start(bf16[2,512,512]{2,1,0:T(8,128)(2,1)} %get-tuple-element.5) | copy-start | bytes 3145732
